TPU v7x, 32 devices: a whole 2x2x4 slice. The times are simulated.
32 devices in a mesh: groups: 2 (over x), expert: 16 (over z, y, core).
Axes of the slice: x: 2, y: 2, z: 4, core: 2. Of those that a mesh axis runs over, the one named last changes fastest.
Arguments:
- tokens: bfloat16 [4096, 4096], P(('groups', 'expert')), parts along dimension 0, may hold values from -6 to 6
- cotangent: bfloat16 [4096, 4096], P(('groups', 'expert')), parts along dimension 0, may hold values from -6 to 6
- gate_weight: bfloat16 [4096, 16384], P(None, 'expert'), may hold values from -0.09375 to 0.09375
- up_weight: bfloat16 [4096, 16384], P(None, 'expert'), may hold values from -0.09375 to 0.09375
- down_weight: bfloat16 [16384, 4096], P('expert'), may hold values from -0.0625 to 0.0625
- chosen: int32 [4, 64], P('groups'), parts along dimension 0, may hold values from 0 to 2047, as said below
- counts: int32 [4], P('groups'), parts along dimension 0, may hold values from 8 to 64, as said below
- gate_values: float32 [4, 64], P('groups'), parts along dimension 0, may hold values from 0.1 to 1
Outputs:
- layer_out: bfloat16 [4096, 4096], P(('groups', 'expert')), parts along dimension 0
- token_grad: bfloat16 [4096, 4096], P(('groups', 'expert')), parts along dimension 0
- gate_grad: float32 [4, 64], P('groups'), parts along dimension 0
There are 2 independent parts, one for each index of `groups`. A program takes and returns all parts, laid end to end along the dimension named above; an argument that names none is the same for every part. Nothing has to cross between parts.
Inputs may be any that keep to these rules, and one draw needn't show every extreme that they name: `chosen`: in each of the 2 rows the first counts[e] entries are distinct token indices in increasing order; at most 8 of them lie among the 128 tokens of one device (indices j * 128 to (j + 1) * 128 - 1), and in every draw each expert takes exactly 8 from some device. Entries from counts[e] on are padding with arbitrary values. `counts`: in every draw some expert has all 64 slots valid.
All inputs are finite; a program needn't handle non-finite values.
Results may differ from a plain program's by a relative error of at most 0.0058.
Values may be sent and summed in bfloat16 or wider, within the bound.
A program may use at most 128 MiB of HBM per device.

v0:
```python
import jax
import jax.numpy as jnp
from jax import lax
from jax.sharding import PartitionSpec as P

EXP_FLY = 2
SLOT = 8


def route_back(term_rows, target, group_width, devices):
    owner_slots = jnp.zeros((devices * SLOT, term_rows.shape[1]), jnp.float32)
    owner_slots = owner_slots.at[target].set(term_rows, mode="drop")
    arrived = lax.all_to_all(
        owner_slots.reshape(devices, SLOT, -1), "expert", split_axis=0, concat_axis=0, tiled=True
    )
    return arrived.reshape(EXP_FLY, group_width, SLOT, -1).sum(axis=1)


def shards(tokens, cotangent, gate_weight, up_weight, down_weight, chosen, counts, gate_values):
    devices = lax.axis_size("expert")
    my_index = lax.axis_index("expert")
    group_width = devices // EXP_FLY
    own_expert = my_index // group_width
    tok_rows = tokens.shape[0]
    capacity = chosen.shape[1]
    positions = jnp.arange(capacity, dtype=jnp.int32)
    live_mask = positions[None, :] < counts[:, None]
    owners = chosen // tok_rows
    earlier = jnp.sum(live_mask[:, None, :] & (owners[:, None, :] < owners[:, :, None]), axis=2)
    slot_of = positions[None, :] - earlier
    own_rows = live_mask & (owners == my_index)
    local_tok = chosen - my_index * tok_rows
    slot_hot = (slot_of[:, :, None] == jnp.arange(SLOT)[None, None, :]) & own_rows[:, :, None]
    tok_hot = local_tok[:, :, None] == jnp.arange(tok_rows)[None, None, :]
    pick_table = jnp.einsum(
        "eks,ekt->est",
        slot_hot.astype(jnp.float32),
        tok_hot.astype(jnp.float32),
        precision=lax.Precision.HIGHEST,
    )
    pick_narrow = pick_table.astype(jnp.bfloat16)
    send_tokens = jnp.einsum(
        "est,td->esd", pick_narrow, tokens, preferred_element_type=jnp.float32
    ).astype(jnp.bfloat16)
    send_grads = jnp.einsum(
        "est,td->esd", pick_narrow, cotangent, preferred_element_type=jnp.float32
    ).astype(jnp.bfloat16)
    send_tokens = jnp.repeat(send_tokens, group_width, axis=0)
    send_grads = jnp.repeat(send_grads, group_width, axis=0)
    arrived_tokens, arrived_grads = (
        lax.all_to_all(send_tokens, "expert", split_axis=0, concat_axis=0, tiled=True),
        lax.all_to_all(send_grads, "expert", split_axis=0, concat_axis=0, tiled=True),
    )
    own_live = lax.dynamic_index_in_dim(live_mask, own_expert, 0, keepdims=False)
    own_slot = lax.dynamic_index_in_dim(slot_of, own_expert, 0, keepdims=False)
    own_owner = lax.dynamic_index_in_dim(owners, own_expert, 0, keepdims=False)
    own_gate_row = lax.dynamic_index_in_dim(gate_values, own_expert, 0, keepdims=False)
    own_gate = jnp.where(own_live, own_gate_row, jnp.zeros_like(own_gate_row))
    flat_place = own_owner * SLOT + own_slot
    fetch_place = jnp.where(own_live, flat_place, 0)
    store_place = jnp.where(own_live, flat_place, devices * SLOT)
    expert_rows = jnp.take(arrived_tokens.reshape(devices * SLOT, -1), fetch_place, axis=0)
    pre_gate = jnp.dot(expert_rows, gate_weight, preferred_element_type=jnp.float32)
    pre_up = jnp.dot(expert_rows, up_weight, preferred_element_type=jnp.float32)
    gate_sigmoid = jax.nn.sigmoid(pre_gate)
    activated = pre_gate * gate_sigmoid
    hidden = (activated * pre_up).astype(jnp.bfloat16)
    partial_value = jnp.dot(hidden, down_weight, preferred_element_type=jnp.float32)
    routed_out = route_back(own_gate[:, None] * partial_value, store_place, group_width, devices)
    layer_out = jnp.einsum(
        "est,esd->td", pick_table, routed_out, precision=lax.Precision.HIGHEST
    ).astype(jnp.bfloat16)
    expert_grads = jnp.take(arrived_grads.reshape(devices * SLOT, -1), fetch_place, axis=0)
    local_terms = jnp.sum(partial_value * expert_grads.astype(jnp.float32), axis=1)
    local_terms = jnp.where(own_live, local_terms, jnp.zeros_like(local_terms))
    placed = jnp.where(jnp.arange(EXP_FLY)[:, None] == own_expert, local_terms[None, :], 0.0)
    gate_grad = lax.psum(placed, "expert")
    scaled = (own_gate[:, None] * expert_grads.astype(jnp.float32)).astype(jnp.bfloat16)
    back_hidden = lax.dot_general(
        scaled, down_weight, (((1,), (1,)), ((), ())), preferred_element_type=jnp.float32
    )
    grad_gate_in = (
        back_hidden * pre_up * gate_sigmoid * (1.0 + pre_gate * (1.0 - gate_sigmoid))
    ).astype(jnp.bfloat16)
    grad_up_in = (back_hidden * activated).astype(jnp.bfloat16)
    partial_grad = lax.dot_general(
        grad_gate_in, gate_weight, (((1,), (1,)), ((), ())), preferred_element_type=jnp.float32
    )
    partial_grad = partial_grad + lax.dot_general(
        grad_up_in, up_weight, (((1,), (1,)), ((), ())), preferred_element_type=jnp.float32
    )
    routed_grad = route_back(partial_grad, store_place, group_width, devices)
    token_grad = jnp.einsum(
        "est,esd->td", pick_table, routed_grad, precision=lax.Precision.HIGHEST
    ).astype(jnp.bfloat16)
    return (layer_out, token_grad, gate_grad)


def solution(mesh):
    placed = (
        P(("groups", "expert"), None),
        P(("groups", "expert"), None),
        P(None, "expert"),
        P(None, "expert"),
        P("expert", None),
        P("groups", None),
        P("groups"),
        P("groups", None),
    )
    return jax.shard_map(
        shards,
        mesh=mesh,
        in_specs=placed,
        out_specs=(P(("groups", "expert"), None), P(("groups", "expert"), None), P("groups", None)),
        check_vma=False,
    )
```

profile of v0, /device:TPU:0, one launch (start us, length us, event | category | flops | bytes accessed | tf_op | source)
XLA Modules:
  0.0 215.2 jit_solution(6746835040889019272)
XLA Ops:
  0.6 0.0 copy-start
  0.7 0.9 compare_and_fusion.1
  1.5 0.2 convert_reduce_fusion
  1.7 0.7 iota_subtract_fusion
  2.4 0.2 fusion.21
  2.6 0.2 convolution_convert_fusion.1
  2.8 1.1 broadcast_in_dim.63
  3.9 7.4 %all-to-all-start = ((bf16[16,8,4096]{2,1,0:T(8,128)(2,1)}), bf16[16,8,4096]{2,1,0:T(8,128)(2,1)S(1)}, u32[]{:S(2)}, u32[]{:S(2)}) async-start(bf16[16,8,4096]{2,1,0:T(8,128)(2,1)} %bitcast.5), calls=%async_computation | async-start | bytes 2097152 | tf_op jit(solution)/shard_map/all_to_all | solution.py:51
  11.3 1.5 convolution_convert_fusion
  12.8 21.5 %all-to-all-done = bf16[16,8,4096]{2,1,0:T(8,128)(2,1)S(1)} async-done(((bf16[16,8,4096]{2,1,0:T(8,128)(2,1)}), bf16[16,8,4096]{2,1,0:T(8,128)(2,1)S(1)}, u32[]{:S(2)}, u32[]{:S(2)}) %all-to-all-start) | async-done | bytes 1048608 | tf_op jit(solution)/shard_map/all_to_all | solution.py:51
  34.3 1.1 broadcast_in_dim.64
  35.3 6.9 %all-to-all-start.2 = ((bf16[16,8,4096]{2,1,0:T(8,128)(2,1)}), bf16[16,8,4096]{2,1,0:T(8,128)(2,1)S(1)}, u32[]{:S(2)}, u32[]{:S(2)}) async-start(bf16[16,8,4096]{2,1,0:T(8,128)(2,1)} %bitcast.57), calls=%async_computation.2 | async-start | bytes 2097152 | tf_op jit(solution)/shard_map/all_to_all | solution.py:52
  42.3 1.7 gather_fusion
  44.0 5.2 %fusion.17 = f32[64,1024]{1,0:T(8,128)S(1)} fusion(bf16[4096,1024]{1,0:T(8,128)(2,1)} %param.12, bf16[64,4096]{1,0:T(8,128)(2,1)} %gather_fusion, pred[64]{0:T(512)(128)(4,1)S(1)} %get-tuple-element.6), kind=kOutput, calls=%fused_computation.35 | convolution fusion | flops 537133056 | bytes 9175104 | tf_op jit(solution)/shard_map/dot_general | solution.py:63
  49.2 5.7 %fusion.16 = f32[64,1024]{1,0:T(8,128)} fusion(bf16[4096,1024]{1,0:T(8,128)(2,1)} %param.13, bf16[64,4096]{1,0:T(8,128)(2,1)S(1)} %copy-done.1, pred[64]{0:T(512)(128)(4,1)S(1)} %get-tuple-element.6), kind=kOutput, calls=%fused_computation.34 | convolution fusion | flops 537133056 | bytes 9175104 | tf_op jit(solution)/shard_map/dot_general | solution.py:64
  54.9 10.2 %all-to-all-done.2 = bf16[16,8,4096]{2,1,0:T(8,128)(2,1)S(1)} async-done(((bf16[16,8,4096]{2,1,0:T(8,128)(2,1)}), bf16[16,8,4096]{2,1,0:T(8,128)(2,1)S(1)}, u32[]{:S(2)}, u32[]{:S(2)}) %all-to-all-start.2) | async-done | bytes 1048608 | tf_op jit(solution)/shard_map/all_to_all | solution.py:52
  65.1 0.9 gather_fusion.1
  66.1 6.3 %fusion.11 = f32[64,1024]{1,0:T(8,128)S(1)} fusion(bf16[1024,4096]{1,0:T(8,128)(2,1)} %param.14, f32[64]{0:T(128)S(1)} %get-tuple-element.4, bf16[64,4096]{1,0:T(8,128)(2,1)S(1)} %gather_fusion.1, pred[64]{0:T(512)(128)(4,1)S(1)} %get-tuple-element.6), kind=kOutput, calls=%fused_computation.24 | convolution fusion | flops 537919488 | bytes 9175360 | tf_op jit(solution)/shard_map/dot_general | solution.py:79
  72.4 6.2 %fusion.19 = f32[64,4096]{1,0:T(8,128)S(1)} fusion(bf16[4096,1024]{1,0:T(8,128)(2,1)} %param.12, f32[64,1024]{1,0:T(8,128)S(1)} %fusion.17, f32[64,1024]{1,0:T(8,128)S(1)} %fusion.11, f32[64,1024]{1,0:T(8,128)S(1)} %copy-done.3), kind=kOutput, calls=%fused_computation.37 | convolution fusion | flops 537526272 | bytes 10223616 | tf_op jit(solution)/shard_map/dot_general | solution.py:86
  78.6 3.7 %convolution_add_fusion = f32[64,4096]{1,0:T(8,128)} fusion(f32[64,4096]{1,0:T(8,128)S(1)} %fusion.19, bf16[4096,1024]{1,0:T(8,128)(2,1)S(1)} %bitcast.52, f32[64,1024]{1,0:T(8,128)S(1)} %fusion.11, f32[64,1024]{1,0:T(8,128)S(1)} %fusion.17), kind=kOutput, calls=%fused_computation.8 | convolution fusion | flops 537526272 | bytes 11010048 | tf_op jit(solution)/shard_map/dot_general | solution.py:89
  82.2 3.3 %scatter_custom_fusion.1 = f32[128,4096]{1,0:T(8,128)} fusion(s32[64]{0:T(128)S(1)} %fusion.35, f32[64,4096]{1,0:T(8,128)} %convolution_add_fusion, f32[]{:T(128)} %constant.64.clone.1), kind=kCustom, calls=%fused_computation.21 | custom fusion | bytes 2097664 | tf_op jit(solution)/shard_map/scatter | solution.py:12
  85.5 6.9 %all-to-all-start.3 = ((f32[16,8,4096]{2,1,0:T(8,128)}), f32[16,8,4096]{2,1,0:T(8,128)S(1)}, u32[]{:S(2)}, u32[]{:S(2)}) async-start(f32[16,8,4096]{2,1,0:T(8,128)} %bitcast.56), calls=%async_computation.3 | async-start | bytes 4194304 | tf_op jit(solution)/shard_map/all_to_all | solution.py:13
  92.4 6.1 %fusion.3 = (f32[64]{0:T(128)S(1)}, f32[64,4096]{1,0:T(8,128)}) fusion(bf16[64,4096]{1,0:T(8,128)(2,1)} %copy-done.2, pred[64]{0:T(512)(128)(4,1)S(1)} %get-tuple-element.6, bf16[1024,4096]{1,0:T(8,128)(2,1)} %param.14, f32[64,1024]{1,0:T(8,128)} %fusion.16, f32[64,1024]{1,0:T(8,128)S(1)} %fusion.17), kind=kOutput, calls=%fused_computation.16 | convolution fusion | flops 538312640 | bytes 10486080 | tf_op jit(solution)/shard_map/dot_general | solution.py:68
  98.5 3.4 %scatter_custom_fusion = f32[128,4096]{1,0:T(8,128)} fusion(s32[64]{0:T(128)S(1)} %fusion.35, f32[64,4096]{1,0:T(8,128)} %get-tuple-element.13, f32[]{:T(128)} %constant.64.clone.1, f32[64]{0:T(128)S(1)} %get-tuple-element.4), kind=kCustom, calls=%fused_computation.19 | custom fusion | flops 262144 | bytes 3146244 | tf_op jit(solution)/shard_map/scatter | solution.py:12
  102.0 31.5 %all-to-all-done.3 = f32[16,8,4096]{2,1,0:T(8,128)S(1)} async-done(((f32[16,8,4096]{2,1,0:T(8,128)}), f32[16,8,4096]{2,1,0:T(8,128)S(1)}, u32[]{:S(2)}, u32[]{:S(2)}) %all-to-all-start.3) | async-done | bytes 2097184 | tf_op jit(solution)/shard_map/all_to_all | solution.py:13
  133.5 11.3 %all-to-all-start.1 = ((f32[16,8,4096]{2,1,0:T(8,128)}), f32[16,8,4096]{2,1,0:T(8,128)}, u32[]{:S(2)}, u32[]{:S(2)}) async-start(f32[16,8,4096]{2,1,0:T(8,128)} %bitcast.55), calls=%async_computation.1 | async-start | bytes 4194304 | tf_op jit(solution)/shard_map/all_to_all | solution.py:13
  144.8 0.1 broadcast_select_fusion.5
  144.9 62.9 %psum.7 = f32[2,64]{1,0:T(2,128)} all-reduce(f32[2,64]{1,0:T(2,128)S(1)} %broadcast_select_fusion.5), channel_id=1, replica_groups=mesh['groups'=2,'expert'=16] {'expert'}, use_global_device_ids=true, to_apply=%region_6.8 | all-reduce | flops 128 | bytes 1024 | tf_op jit(solution)/shard_map/psum | solution.py:77
  207.7 0.1 bitcast_reduce_fusion
  207.8 2.8 %fusion.1 = bf16[128,4096]{1,0:T(8,128)(2,1)} fusion(f32[2,8,128]{2,1,0:T(8,128)S(1)} %fusion.21, f32[2,8,4096]{2,1,0:T(8,128)S(1)} %bitcast_reduce_fusion), kind=kOutput, calls=%fused_computation.7 | convolution fusion | flops 101187584 | bytes 1318912 | tf_op jit(solution)/shard_map/est,esd->td/dot_general | solution.py:93
  210.6 1.7 bitcast_reduce_fusion.1
  212.3 2.8 %fusion = bf16[128,4096]{1,0:T(8,128)(2,1)} fusion(f32[2,8,128]{2,1,0:T(8,128)S(1)} %fusion.21, f32[2,8,4096]{2,1,0:T(8,128)S(1)} %bitcast_reduce_fusion.1), kind=kOutput, calls=%fused_computation.6 | convolution fusion | flops 101187584 | bytes 1318912 | tf_op jit(solution)/shard_map/est,esd->td/dot_general | solution.py:70
  (21 shorter events, 0.1 us)
Async XLA Ops:
  0.6 2.0 copy-start
  0.6 41.6 %copy-start.4 = (f32[2,64]{1,0:T(2,128)S(1)}, f32[2,64]{1,0:T(2,128)}, u32[]{:S(2)}) copy-start(f32[2,64]{1,0:T(2,128)} %param.17) | copy-start | bytes 1540
  3.9 30.3 %all-to-all-start = ((bf16[16,8,4096]{2,1,0:T(8,128)(2,1)}), bf16[16,8,4096]{2,1,0:T(8,128)(2,1)S(1)}, u32[]{:S(2)}, u32[]{:S(2)}) async-start(bf16[16,8,4096]{2,1,0:T(8,128)(2,1)} %bitcast.5), calls=%async_computation | async-start | bytes 2097152 | tf_op jit(solution)/shard_map/all_to_all | solution.py:51
  35.3 29.8 %all-to-all-start.2 = ((bf16[16,8,4096]{2,1,0:T(8,128)(2,1)}), bf16[16,8,4096]{2,1,0:T(8,128)(2,1)S(1)}, u32[]{:S(2)}, u32[]{:S(2)}) async-start(bf16[16,8,4096]{2,1,0:T(8,128)(2,1)} %bitcast.57), calls=%async_computation.2 | async-start | bytes 2097152 | tf_op jit(solution)/shard_map/all_to_all | solution.py:52
  44.0 5.2 %copy-start.1 = (bf16[64,4096]{1,0:T(8,128)(2,1)S(1)}, bf16[64,4096]{1,0:T(8,128)(2,1)}, u32[]{:S(2)}) copy-start(bf16[64,4096]{1,0:T(8,128)(2,1)} %gather_fusion) | copy-start | bytes 1572868
  66.0 12.5 %copy-start.2 = (bf16[64,4096]{1,0:T(8,128)(2,1)}, bf16[64,4096]{1,0:T(8,128)(2,1)S(1)}, u32[]{:S(2)}) copy-start(bf16[64,4096]{1,0:T(8,128)(2,1)S(1)} %gather_fusion.1) | copy-start | bytes 1572868
  66.0 6.3 %copy-start.3 = (f32[64,1024]{1,0:T(8,128)S(1)}, f32[64,1024]{1,0:T(8,128)}, u32[]{:S(2)}) copy-start(f32[64,1024]{1,0:T(8,128)} %fusion.16) | copy-start | bytes 786436
  66.0 12.5 %slice-start = ((s8[8388608]{0:T(1024)(128)(4,1)}), s8[4194304]{0:T(1024)(128)(4,1)S(1)}, s32[]{:S(2)}) async-start(s8[8388608]{0:T(1024)(128)(4,1)} %bitcast.51), calls=%async_computation.4 | async-start | bytes 8388608
  72.3 6.2 %slice-start.1 = ((s8[8388608]{0:T(1024)(128)(4,1)}), s8[4194304]{0:T(1024)(128)(4,1)S(1)}, s32[]{:S(2)}) async-start(s8[8388608]{0:T(1024)(128)(4,1)} %bitcast.51), calls=%async_computation.5 | async-start | bytes 8388608
  85.5 48.0 %all-to-all-start.3 = ((f32[16,8,4096]{2,1,0:T(8,128)}), f32[16,8,4096]{2,1,0:T(8,128)S(1)}, u32[]{:S(2)}, u32[]{:S(2)}) async-start(f32[16,8,4096]{2,1,0:T(8,128)} %bitcast.56), calls=%async_computation.3 | async-start | bytes 4194304 | tf_op jit(solution)/shard_map/all_to_all | solution.py:13
  133.5 77.1 %all-to-all-start.1 = ((f32[16,8,4096]{2,1,0:T(8,128)}), f32[16,8,4096]{2,1,0:T(8,128)}, u32[]{:S(2)}, u32[]{:S(2)}) async-start(f32[16,8,4096]{2,1,0:T(8,128)} %bitcast.55), calls=%async_computation.1 | async-start | bytes 4194304 | tf_op jit(solution)/shard_map/all_to_all | solution.py:13
where the time goes:
time: 218 us; the launch traced here: 215 us
  waiting for transfers between devices  63.2 us (29%)
  blocking collectives  62.9 us (29%)
  matrix products  40.7 us (19%)
  starting transfers between devices  32.4 us (15%)
  local copies, waits for them, and re-layouts  7.99 us (4%)
  other arithmetic  7.09 us (3%)
    psum x1, blocking collectives, shards(): gate_grad = lax.psum(placed, 'expert')  62.9 us
    all_to_all x2, waiting for transfers between devices, route_back(): lax.all_to_all(owner_slots.reshape(devices, SLOT, -1), 'expert', split_ax...  31.5 us
    all_to_all x1, waiting for transfers between devices, shards(): lax.all_to_all(send_tokens, 'expert', split_axis=0, concat_axis=0, tiled=...  21.5 us
    all_to_all x2, starting transfers between devices, route_back(): lax.all_to_all(owner_slots.reshape(devices, SLOT, -1), 'expert', split_ax...  18.1 us
    all_to_all x1, waiting for transfers between devices, shards(): lax.all_to_all(send_grads, 'expert', split_axis=0, concat_axis=0, tiled=T...  10.2 us
    all_to_all x1, starting transfers between devices, shards(): lax.all_to_all(send_tokens, 'expert', split_axis=0, concat_axis=0, tiled=...  7.39 us
    all_to_all x1, starting transfers between devices, shards(): lax.all_to_all(send_grads, 'expert', split_axis=0, concat_axis=0, tiled=T...  6.86 us
    dot_general x1, matrix products, shards(): lax.dot_general(scaled, down_weight, (((1,), (1,)), ((), ())), preferred_...  6.27 us
  transfers between devices with their start and end apart: 4, of which 3 were waited for; matrix products, arithmetic and copies ran while one was open for 12% of the time, Pallas kernels for 0%

commit v1 on v0

v1 whole, which is shorter than its diff:
```python
import functools

import jax
import jax.numpy as jnp
from jax import lax
from jax.experimental import pallas as pl
from jax.experimental.pallas import tpu as pltpu
from jax.sharding import PartitionSpec as P

SLOT = 8
PAIR = 2 * SLOT
FAR = 1e9
F32 = jnp.float32
BF16 = jnp.bfloat16


def dot(a, b):
    return jnp.dot(a, b, preferred_element_type=F32)


def dot_nt(a, b):
    return lax.dot_general(a, b, (((1,), (1,)), ((), ())), preferred_element_type=F32)


def iota(shape, axis):
    return lax.broadcasted_iota(jnp.int32, shape, axis)


def hot(mask):
    return jnp.where(mask, 1.0, 0.0).astype(F32)


def kernel(
    n, experts, packed,
    tok_hbm, cot_hbm, wg_hbm, wu_hbm, wd_hbm, chosen_ref, counts_ref, gate_ref,
    out_ref, grad_ref, gg_ref,
    tok_v, cot_v, wg_v, wu_v, wd_v, send_a, land_a, rows_t, rows_g, acc_g, acc_u, acc_b, gg_acc,
    rs_send_v, rs_send_g, rs_v, rs_g, own_send_v, own_send_g, own_v, own_g, gg_send, gg_land,
    loc_sem, wg_sem, wu_sem, wd_sem,
    a_ss, a_rs, bt_ss, bt_rs, bg_ss, bg_rs, rv_ss, rv_rs, rg_ss, rg_rs, ov_ss, ov_rs, og_ss, og_rs, q_ss, q_rs,
):
    gw = n // experts
    me = lax.axis_index("expert")
    my_e = me // gw
    my_c = me % gw
    base = my_e * gw
    tok = tok_v.shape[0]
    chunk = rows_t.shape[2]
    cap = rows_t.shape[1]
    capl = gg_send.shape[1]

    def other(i):
        return lax.rem(me + i, n)

    def back(i):
        return lax.rem(me + n - i, n)

    def ring(i):
        return lax.rem(my_c + i, gw)

    def ring_back(i):
        return lax.rem(my_c + gw - i, gw)

    def remote(src, dst, ss, rs, to):
        return pltpu.make_async_remote_copy(
            src_ref=src, dst_ref=dst, send_sem=ss, recv_sem=rs,
            device_id={"expert": to}, device_id_type=pl.DeviceIdType.MESH,
        )

    tok_copy = pltpu.make_async_copy(tok_hbm, tok_v, loc_sem.at[0])
    cot_copy = pltpu.make_async_copy(cot_hbm, cot_v, loc_sem.at[1])
    tok_copy.start()
    cot_copy.start()

    def wg_copy(c):
        at = pl.multiple_of(c * chunk, chunk)
        return pltpu.make_async_copy(wg_hbm.at[pl.ds(at, chunk), :], wg_v.at[c], wg_sem.at[c])

    def wu_copy(c):
        at = pl.multiple_of(c * chunk, chunk)
        return pltpu.make_async_copy(wu_hbm.at[pl.ds(at, chunk), :], wu_v.at[c], wu_sem.at[c])

    def wd_copy(c):
        at = pl.multiple_of(c * chunk, chunk)
        return pltpu.make_async_copy(wd_hbm.at[:, pl.ds(at, chunk)], wd_v.at[c], wd_sem.at[c])

    barrier = pltpu.get_barrier_semaphore()

    @pl.loop(1, n)
    def _(i):
        pl.semaphore_signal(barrier, inc=1, device_id={"expert": other(i)}, device_id_type=pl.DeviceIdType.MESH)

    @pl.loop(0, gw)
    def _(i):
        c = ring_back(i)
        wg_copy(c).start()
        wu_copy(c).start()

    @pl.loop(0, gw)
    def _(i):
        wd_copy(ring(i)).start()

    k_row = iota((1, cap), 1)
    eye = iota((cap, cap), 0) == iota((cap, cap), 1)

    def table(e):
        row = jnp.where(k_row < counts_ref[e], chosen_ref[pl.ds(e, 1), :].astype(F32), FAR)
        col = jnp.sum(jnp.where(eye, row, 0.0), axis=1, keepdims=True)
        return row, col

    first = (me * tok).astype(F32)
    span = float(tok)
    pick = jnp.zeros((experts * SLOT, tok), F32)
    spread = jnp.zeros((tok, experts * SLOT), F32)
    for e in range(experts):
        row, col = table(e)
        start = jnp.sum(hot(row < first), axis=1, keepdims=True)
        j_col = iota((experts * SLOT, cap), 0) - e * SLOT
        j_row = iota((cap, experts * SLOT), 1) - e * SLOT
        a = hot((iota((experts * SLOT, cap), 1).astype(F32) == start + j_col.astype(F32)) & (j_col >= 0) & (j_col < SLOT))
        at = hot((iota((cap, experts * SLOT), 0).astype(F32) == start + j_row.astype(F32)) & (j_row >= 0) & (j_row < SLOT))
        b = hot(col == first + iota((cap, tok), 1).astype(F32))
        bt = hot(row == first + iota((tok, cap), 0).astype(F32))
        pick = pick + dot(a.astype(BF16), b.astype(BF16))
        spread = spread + dot(bt.astype(BF16), at.astype(BF16))
    pick = pick.astype(BF16)
    spread = spread.astype(BF16)

    row, col = table(my_e)
    j = iota((cap, n * PAIR), 1)
    dev = (j // PAIR).astype(F32) * span
    slot = j % PAIR
    start = jnp.sum(hot(col < dev), axis=0, keepdims=True)
    inside = col < dev + span
    k_col = iota((cap, n * PAIR), 0).astype(F32)
    from_t = hot(inside & (slot < SLOT) & (k_col == start + slot.astype(F32))).astype(BF16)
    from_g = hot(inside & (slot >= SLOT) & (k_col == start + (slot - SLOT).astype(F32))).astype(BF16)
    j8 = iota((n * SLOT, cap), 0)
    dev8 = (j8 // SLOT).astype(F32) * span
    start8 = jnp.sum(hot(row < dev8), axis=1, keepdims=True)
    to_slot = hot(
        (row < dev8 + span) & (iota((n * SLOT, cap), 1).astype(F32) == start8 + (j8 % SLOT).astype(F32))
    ).astype(BF16)
    weight_row = jnp.where(k_row < counts_ref[my_e], gate_ref[pl.ds(my_e, 1), :], 0.0)
    weight = jnp.sum(jnp.where(eye, weight_row, 0.0), axis=1, keepdims=True)
    live_row = k_row < counts_ref[my_e]
    live = jnp.sum(jnp.where(eye, hot(live_row), 0.0), axis=1, keepdims=True)

    tok_copy.wait()
    cot_copy.wait()

    @pl.loop(0, gw)
    def _(c):
        cols = pl.ds(pl.multiple_of(c * chunk, chunk), chunk)
        t = dot(pick, tok_v[:, cols])
        g = dot(pick, cot_v[:, cols])
        for e in range(experts):
            lo = e * SLOT
            send_a[e * gw + c] = jnp.concatenate([t[lo:lo + SLOT], g[lo:lo + SLOT]], axis=0).astype(BF16)

    pl.semaphore_wait(barrier, n - 1)

    def a_copy(to, slot_of):
        return remote(send_a.at[to], land_a.at[slot_of], a_ss.at[to], a_rs.at[slot_of], to)

    @pl.loop(1, n)
    def _(i):
        a_copy(other(i), me).start()

    land_a[me] = send_a[me]

    @pl.loop(1, n)
    def _(i):
        a_copy(me, back(i)).wait_recv()

    arrived = land_a[...].reshape(n * PAIR, chunk)
    rows_t[my_c] = dot(from_t, arrived).astype(BF16)

    def bt_copy(to, at):
        return remote(rows_t.at[at], rows_t.at[at], bt_ss.at[to], bt_rs.at[at], base + to)

    def bg_copy(to, at):
        return remote(rows_g.at[at], rows_g.at[at], bg_ss.at[to], bg_rs.at[at], base + to)

    @pl.loop(1, gw)
    def _(i):
        bt_copy(ring(i), my_c).start()

    rows_g[my_c] = dot(from_g, arrived).astype(BF16)

    @pl.loop(1, gw)
    def _(i):
        bg_copy(ring(i), my_c).start()

    wg_copy(my_c).wait()
    wu_copy(my_c).wait()
    acc_g[...] = dot(rows_t[my_c], wg_v[my_c])
    acc_u[...] = dot(rows_t[my_c], wu_v[my_c])

    @pl.loop(1, gw)
    def _(i):
        c = ring_back(i)
        bt_copy(my_c, c).wait_recv()
        wg_copy(c).wait()
        wu_copy(c).wait()
        x = rows_t[c]
        acc_g[...] += dot(x, wg_v[c])
        acc_u[...] += dot(x, wu_v[c])

    pre_gate = acc_g[...]
    hidden = (pre_gate * jax.nn.sigmoid(pre_gate) * acc_u[...]).astype(BF16)

    def rv_copy(to, at):
        return remote(rs_send_v.at[to], rs_v.at[at], rv_ss.at[to], rv_rs.at[at], base + to)

    def rg_copy(to, at):
        return remote(rs_send_g.at[to], rs_g.at[at], rg_ss.at[to], rg_rs.at[at], base + to)

    gg_acc[...] = jnp.zeros_like(gg_acc)

    @pl.loop(1, gw)
    def _(i):
        c = ring(i)
        bg_copy(my_c, c).wait_recv()
        wd_copy(c).wait()
        value = dot(hidden, wd_v[c])
        rs_send_v[c] = value.astype(BF16)
        rv_copy(c, my_c).start()
        gg_acc[...] += value * rows_g[c].astype(F32)

    wd_copy(my_c).wait()
    value = dot(hidden, wd_v[my_c])
    rs_v[my_c] = value.astype(BF16)
    terms = live * jnp.sum(gg_acc[...] + value * rows_g[my_c].astype(F32), axis=1, keepdims=True)
    wide = iota((cap, capl), 0) == iota((cap, capl), 1)
    gg_send[...] = jnp.broadcast_to(jnp.sum(jnp.where(wide, terms, 0.0), axis=0, keepdims=True), gg_send.shape)

    def q_copy(to, at):
        return remote(gg_send, gg_land.at[at], q_ss.at[to], q_rs.at[at], to)

    @pl.loop(1, n)
    def _(i):
        q_copy(other(i), me).start()

    gg_land[me] = gg_send[...]

    acc_b[...] = jnp.zeros_like(acc_b)

    @pl.loop(0, gw)
    def _(c):
        scaled = (weight * rows_g[c].astype(F32)).astype(BF16)
        acc_b[...] += dot_nt(scaled, wd_v[c])

    up = acc_u[...]
    sig = jax.nn.sigmoid(pre_gate)
    backed = acc_b[...]
    d_gate = (backed * up * sig * (1.0 + pre_gate * (1.0 - sig))).astype(BF16)
    d_up = (backed * (pre_gate * sig)).astype(BF16)

    def to_owners(term, buf):
        slots = dot(to_slot, term.astype(BF16)).reshape(n, SLOT, chunk)
        if packed:
            half = chunk // 2
            slots = jnp.concatenate([slots[:, :, :half], slots[:, :, half:]], axis=1).astype(BF16)
        buf[...] = slots

    def summed(buf):
        return lax.fori_loop(1, gw, lambda c, s: s + buf[c].astype(F32), buf[0].astype(F32))

    def ov_copy(to, at):
        return remote(own_send_v.at[to], own_v.at[at], ov_ss.at[to], ov_rs.at[at], to)

    def og_copy(to, at):
        return remote(own_send_g.at[to], own_g.at[at], og_ss.at[to], og_rs.at[at], to)

    @pl.loop(1, gw)
    def _(i):
        rv_copy(my_c, ring_back(i)).wait_recv()

    to_owners(weight * summed(rs_v), own_send_v)

    @pl.loop(1, n)
    def _(i):
        ov_copy(other(i), me).start()

    own_v[me] = own_send_v[me]

    @pl.loop(1, gw)
    def _(i):
        c = ring(i)
        rs_send_g[c] = (dot_nt(d_gate, wg_v[c]) + dot_nt(d_up, wu_v[c])).astype(BF16)
        rg_copy(c, my_c).start()

    rs_g[my_c] = (dot_nt(d_gate, wg_v[my_c]) + dot_nt(d_up, wu_v[my_c])).astype(BF16)

    @pl.loop(1, gw)
    def _(i):
        rg_copy(my_c, ring_back(i)).wait_recv()

    to_owners(summed(rs_g), own_send_g)

    @pl.loop(1, n)
    def _(i):
        og_copy(other(i), me).start()

    own_g[me] = own_send_g[me]

    def unpack(x):
        x = x.astype(F32)
        if packed:
            x = jnp.concatenate([x[:SLOT], x[SLOT:]], axis=1)
        return x

    def finish(buf, ref):
        @pl.loop(0, gw)
        def _(c):
            rows = jnp.concatenate([unpack(buf[e * gw + c]) for e in range(experts)], axis=0)
            cols = pl.ds(pl.multiple_of(c * chunk, chunk), chunk)
            ref[:, cols] = dot(spread, rows.astype(BF16)).astype(BF16)

    @pl.loop(1, n)
    def _(i):
        ov_copy(me, back(i)).wait_recv()

    finish(own_v, out_ref)

    @pl.loop(1, n)
    def _(i):
        q_copy(me, back(i)).wait_recv()

    for e in range(experts):
        total = lax.fori_loop(1, gw, lambda c, s: s + gg_land[e * gw + c], gg_land[e * gw])
        gg_ref[e:e + 1, :] = total[0:1, :cap]

    @pl.loop(1, n)
    def _(i):
        og_copy(me, back(i)).wait_recv()

    finish(own_g, grad_ref)

    @pl.loop(1, n)
    def _(i):
        to = other(i)
        a_copy(to, me).wait_send()
        q_copy(to, me).wait_send()
        ov_copy(to, me).wait_send()
        og_copy(to, me).wait_send()

    @pl.loop(1, gw)
    def _(i):
        to = ring(i)
        bt_copy(to, my_c).wait_send()
        bg_copy(to, my_c).wait_send()
        rv_copy(to, my_c).wait_send()
        rg_copy(to, my_c).wait_send()


def shards(tokens, cotangent, gate_weight, up_weight, down_weight, chosen, counts, gate_values):
    n = lax.axis_size("expert")
    experts, cap = chosen.shape
    gw = n // experts
    tok, d = tokens.shape
    ff = gate_weight.shape[1]
    chunk = d // gw
    capl = -(-cap // 128) * 128
    packed = chunk % 256 == 0
    own_shape = (n, PAIR, chunk // 2) if packed else (n, SLOT, chunk)
    own_type = BF16 if packed else F32
    vmem = pl.BlockSpec(memory_space=pltpu.VMEM)
    hbm = pl.BlockSpec(memory_space=pl.ANY)
    dma = pltpu.SemaphoreType.DMA
    return pl.pallas_call(
        functools.partial(kernel, n, experts, packed),
        out_shape=(
            jax.ShapeDtypeStruct((tok, d), BF16),
            jax.ShapeDtypeStruct((tok, d), BF16),
            jax.ShapeDtypeStruct((experts, cap), F32),
        ),
        in_specs=[hbm] * 5 + [vmem, pl.BlockSpec(memory_space=pltpu.SMEM), vmem],
        out_specs=(vmem, vmem, vmem),
        scratch_shapes=[
            pltpu.VMEM((tok, d), BF16),
            pltpu.VMEM((tok, d), BF16),
            pltpu.VMEM((gw, chunk, ff), BF16),
            pltpu.VMEM((gw, chunk, ff), BF16),
            pltpu.VMEM((gw, ff, chunk), BF16),
            pltpu.VMEM((n, PAIR, chunk), BF16),
            pltpu.VMEM((n, PAIR, chunk), BF16),
            pltpu.VMEM((gw, cap, chunk), BF16),
            pltpu.VMEM((gw, cap, chunk), BF16),
            pltpu.VMEM((cap, ff), F32),
            pltpu.VMEM((cap, ff), F32),
            pltpu.VMEM((cap, ff), F32),
            pltpu.VMEM((cap, chunk), F32),
            pltpu.VMEM((gw, cap, chunk), BF16),
            pltpu.VMEM((gw, cap, chunk), BF16),
            pltpu.VMEM((gw, cap, chunk), BF16),
            pltpu.VMEM((gw, cap, chunk), BF16),
            pltpu.VMEM(own_shape, own_type),
            pltpu.VMEM(own_shape, own_type),
            pltpu.VMEM(own_shape, own_type),
            pltpu.VMEM(own_shape, own_type),
            pltpu.VMEM((8, capl), F32),
            pltpu.VMEM((n, 8, capl), F32),
            dma((2,)), dma((gw,)), dma((gw,)), dma((gw,)),
            dma((n,)), dma((n,)),
            dma((gw,)), dma((gw,)), dma((gw,)), dma((gw,)),
            dma((gw,)), dma((gw,)), dma((gw,)), dma((gw,)),
            dma((n,)), dma((n,)), dma((n,)), dma((n,)), dma((n,)), dma((n,)),
        ],
        compiler_params=pltpu.CompilerParams(
            collective_id=0, has_side_effects=True, vmem_limit_bytes=56 * 1024 * 1024
        ),
        name="expert_layer",
    )(tokens, cotangent, gate_weight, up_weight, down_weight, chosen, counts, gate_values)


def solution(mesh):
    placed = (
        P(("groups", "expert"), None),
        P(("groups", "expert"), None),
        P(None, "expert"),
        P(None, "expert"),
        P("expert", None),
        P("groups", None),
        P("groups"),
        P("groups", None),
    )
    return jax.shard_map(
        shards,
        mesh=mesh,
        in_specs=placed,
        out_specs=(P(("groups", "expert"), None), P(("groups", "expert"), None), P("groups", None)),
        check_vma=False,
    )
```

time: 218 us -> 62.3 us (0.29); the launches traced: 215 us -> 62 us
  waiting for transfers between devices: 63.2 us -> 0 us
  blocking collectives: 62.9 us -> 0 us
  Pallas kernels: 0 us -> 55.6 us
  matrix products: 40.7 us -> 0 us
  starting transfers between devices: 32.4 us -> 0 us
  other arithmetic: 7.09 us -> 0 us
  local copies, waits for them, and re-layouts: 7.99 us -> 5.8 us
    all_to_all x4 -> x0, waiting for transfers between devices: 63.2 us -> none  [the longest x2 31.5 us: route_back(): lax.all_to_all(owner_slots.reshape(devices, SLOT, -1), 'expert', split_ax...]
    psum x1 -> x0, blocking collectives: 62.9 us -> none  [shards(): gate_grad = lax.psum(placed, 'expert')]
    pallas_call x0 -> x1, Pallas kernels: none -> 55.6 us  [shards(): pl.pallas_call(functools.partial(kernel, n, experts, packed), out_shape=(...]
    dot_general x11 -> x0, matrix products: 40.7 us -> none  [the longest x1 6.27 us: shards(): lax.dot_general(scaled, down_weight, (((1,), (1,)), ((), ())), preferred_...]
    all_to_all x4 -> x0, starting transfers between devices: 32.4 us -> none  [the longest x2 18.1 us: route_back(): lax.all_to_all(owner_slots.reshape(devices, SLOT, -1), 'expert', split_ax...]
    unnamed x14 -> x3, local copies, waits for them, and re-layouts: 0.04 us -> 5.8 us
    scatter x1 -> x0, other arithmetic: 3.42 us -> none  [route_back(): owner_slots = owner_slots.at[target].set(term_rows, mode='drop')]
    scatter x1 -> x0, local copies, waits for them, and re-layouts: 3.26 us -> none  [route_back(): owner_slots = owner_slots.at[target].set(term_rows, mode='drop')]
  transfers between devices with their start and end apart: 4 -> 0, of which waited for: 3 -> 0; matrix products, arithmetic and copies ran while one was open for 12% -> 0% of each run, Pallas kernels for 0% -> 0%
where the time goes in v1:
time: 62.3 us; the launch traced here: 62 us
  Pallas kernels  55.6 us (89%)
  local copies, waits for them, and re-layouts  5.8 us (9%)
  between operations  0.64 us (1%)
    pallas_call x1, Pallas kernels, shards(): pl.pallas_call(functools.partial(kernel, n, experts, packed), out_shape=(...  55.6 us
    unnamed x3, local copies, waits for them, and re-layouts  5.8 us

profile of v1, /device:TPU:0, one launch (start us, length us, event | category | flops | bytes accessed | tf_op | source)
XLA Modules:
  0.0 62.0 jit_solution(8319281365801482774)
XLA Ops:
  0.6 55.6 %expert_layer.1 = (bf16[128,4096]{1,0:T(8,128)(2,1)}, bf16[128,4096]{1,0:T(8,128)(2,1)}, f32[2,64]{1,0:T(2,128)}) custom-call(bf16[128,4096]{1,0:T(8,128)(2,1)} %tok_hbm.1, bf16[128,4096]{1,0:T(8,128)(2,1)} %cot_hbm.1, bf16[4096,1024]{1,0:T(8,128)(2,1)} %wg_hbm.1, bf16[4096,1024]{1,0:T(8,128)(2,1)} %wu_hbm.1, bf16[1024,4096]{1,0:T(8,128)(2,1)} %wd_hbm.1, ...), custom_call_target="tpu_custom_call" | custom-call | tf_op jit(solution)/shard_map/expert_layer/pallas_call | solution.py:372
  56.2 2.3 %copy.14 = bf16[128,4096]{1,0:T(8,128)(2,1)} copy(bf16[128,4096]{1,0:T(8,128)(2,1)} %get-tuple-element.6) | data formatting | bytes 2097152
  58.5 2.3 %copy.15 = bf16[128,4096]{1,0:T(8,128)(2,1)} copy(bf16[128,4096]{1,0:T(8,128)(2,1)} %get-tuple-element.7) | data formatting | bytes 2097152
  60.8 1.2 %copy.16 = f32[2,64]{1,0:T(2,128)} copy(f32[2,64]{1,0:T(2,128)} %get-tuple-element.8) | data formatting | bytes 1024

commit v2 on v1

--- a/solution.py
+++ b/solution.py
@@ -33,16 +33,20 @@
 def kernel(
     n, experts, packed,
     tok_hbm, cot_hbm, wg_hbm, wu_hbm, wd_hbm, chosen_ref, counts_ref, gate_ref,
-    out_ref, grad_ref, gg_ref,
+    out_ref, grad_ref, spread_ref, gg_ref,
     tok_v, cot_v, wg_v, wu_v, wd_v, send_a, land_a, rows_t, rows_g, acc_g, acc_u, acc_b, gg_acc,
-    rs_send_v, rs_send_g, rs_v, rs_g, own_send_v, own_send_g, own_v, own_g, gg_send, gg_land,
+    rs_send_v, rs_send_g, sib_v, sib_g, rs_v, rs_g, own_send_v, own_send_g, own_v, own_g, gg_send, gg_land,
     loc_sem, wg_sem, wu_sem, wd_sem,
-    a_ss, a_rs, bt_ss, bt_rs, bg_ss, bg_rs, rv_ss, rv_rs, rg_ss, rg_rs, ov_ss, ov_rs, og_ss, og_rs, q_ss, q_rs,
+    a_ss, a_rs, bt_ss, bt_rs, bg_ss, bg_rs, rv_ss, sv_rs, rv_rs, rg_ss, sg_rs, rg_rs, ov_ss, ov_rs, og_ss, og_rs, q_ss, q_rs,
 ):
     gw = n // experts
     me = lax.axis_index("expert")
     my_e = me // gw
     my_c = me % gw
+    chips = gw // 2
+    my_chip = my_c // 2
+    core = my_c % 2
+    sib = my_chip * 2 + 1 - core
     base = my_e * gw
     tok = tok_v.shape[0]
     chunk = rows_t.shape[2]
@@ -61,6 +65,15 @@
     def ring_back(i):
         return lax.rem(my_c + gw - i, gw)
 
+    def near(i):
+        return lax.rem(my_chip + i, chips) * 2 + core
+
+    def near_back(i):
+        return lax.rem(my_chip + chips - i, chips) * 2 + core
+
+    def twin(c):
+        return c + 1 - 2 * core
+
     def remote(src, dst, ss, rs, to):
         return pltpu.make_async_remote_copy(
             src_ref=src, dst_ref=dst, send_sem=ss, recv_sem=rs,
@@ -111,20 +124,37 @@
     first = (me * tok).astype(F32)
     span = float(tok)
     pick = jnp.zeros((experts * SLOT, tok), F32)
-    spread = jnp.zeros((tok, experts * SLOT), F32)
     for e in range(experts):
         row, col = table(e)
         start = jnp.sum(hot(row < first), axis=1, keepdims=True)
         j_col = iota((experts * SLOT, cap), 0) - e * SLOT
-        j_row = iota((cap, experts * SLOT), 1) - e * SLOT
         a = hot((iota((experts * SLOT, cap), 1).astype(F32) == start + j_col.astype(F32)) & (j_col >= 0) & (j_col < SLOT))
-        at = hot((iota((cap, experts * SLOT), 0).astype(F32) == start + j_row.astype(F32)) & (j_row >= 0) & (j_row < SLOT))
         b = hot(col == first + iota((cap, tok), 1).astype(F32))
-        bt = hot(row == first + iota((tok, cap), 0).astype(F32))
         pick = pick + dot(a.astype(BF16), b.astype(BF16))
-        spread = spread + dot(bt.astype(BF16), at.astype(BF16))
     pick = pick.astype(BF16)
-    spread = spread.astype(BF16)
+
+    tok_copy.wait()
+    cot_copy.wait()
+
+    @pl.loop(0, gw)
+    def _(c):
+        cols = pl.ds(pl.multiple_of(c * chunk, chunk), chunk)
+        t = dot(pick, tok_v[:, cols])
+        g = dot(pick, cot_v[:, cols])
+        for e in range(experts):
+            lo = e * SLOT
+            send_a[e * gw + c] = jnp.concatenate([t[lo:lo + SLOT], g[lo:lo + SLOT]], axis=0).astype(BF16)
+
+    pl.semaphore_wait(barrier, n - 1)
+
+    def a_copy(to, slot_of):
+        return remote(send_a.at[to], land_a.at[slot_of], a_ss.at[to], a_rs.at[slot_of], to)
+
+    @pl.loop(1, n)
+    def _(i):
+        a_copy(other(i), me).start()
+
+    land_a[me] = send_a[me]
 
     row, col = table(my_e)
     j = iota((cap, n * PAIR), 1)
@@ -145,29 +175,15 @@
     weight = jnp.sum(jnp.where(eye, weight_row, 0.0), axis=1, keepdims=True)
     live_row = k_row < counts_ref[my_e]
     live = jnp.sum(jnp.where(eye, hot(live_row), 0.0), axis=1, keepdims=True)
-
-    tok_copy.wait()
-    cot_copy.wait()
-
-    @pl.loop(0, gw)
-    def _(c):
-        cols = pl.ds(pl.multiple_of(c * chunk, chunk), chunk)
-        t = dot(pick, tok_v[:, cols])
-        g = dot(pick, cot_v[:, cols])
-        for e in range(experts):
-            lo = e * SLOT
-            send_a[e * gw + c] = jnp.concatenate([t[lo:lo + SLOT], g[lo:lo + SLOT]], axis=0).astype(BF16)
-
-    pl.semaphore_wait(barrier, n - 1)
-
-    def a_copy(to, slot_of):
-        return remote(send_a.at[to], land_a.at[slot_of], a_ss.at[to], a_rs.at[slot_of], to)
-
-    @pl.loop(1, n)
-    def _(i):
-        a_copy(other(i), me).start()
-
-    land_a[me] = send_a[me]
+    spread = jnp.zeros((tok, experts * SLOT), F32)
+    for e in range(experts):
+        row, _ = table(e)
+        start = jnp.sum(hot(row < first), axis=1, keepdims=True)
+        j_row = iota((cap, experts * SLOT), 1) - e * SLOT
+        at = hot((iota((cap, experts * SLOT), 0).astype(F32) == start + j_row.astype(F32)) & (j_row >= 0) & (j_row < SLOT))
+        bt = hot(row == first + iota((tok, cap), 0).astype(F32))
+        spread = spread + dot(bt.astype(BF16), at.astype(BF16))
+    spread_ref[...] = spread.astype(BF16)
 
     @pl.loop(1, n)
     def _(i):
@@ -176,61 +192,96 @@
     arrived = land_a[...].reshape(n * PAIR, chunk)
     rows_t[my_c] = dot(from_t, arrived).astype(BF16)
 
-    def bt_copy(to, at):
-        return remote(rows_t.at[at], rows_t.at[at], bt_ss.at[to], bt_rs.at[at], base + to)
-
-    def bg_copy(to, at):
-        return remote(rows_g.at[at], rows_g.at[at], bg_ss.at[to], bg_rs.at[at], base + to)
-
-    @pl.loop(1, gw)
-    def _(i):
-        bt_copy(ring(i), my_c).start()
-
+    def bt_copy(to, at, sem):
+        return remote(rows_t.at[at], rows_t.at[at], bt_ss.at[sem], bt_rs.at[at], base + to)
+
+    def bg_copy(to, at, sem):
+        return remote(rows_g.at[at], rows_g.at[at], bg_ss.at[sem], bg_rs.at[at], base + to)
+
+    @pl.loop(1, chips)
+    def _(i):
+        c = near(i)
+        bt_copy(c, my_c, c).start()
+
+    bt_copy(sib, my_c, sib).start()
     rows_g[my_c] = dot(from_g, arrived).astype(BF16)
 
-    @pl.loop(1, gw)
-    def _(i):
-        bg_copy(ring(i), my_c).start()
-
-    wg_copy(my_c).wait()
-    wu_copy(my_c).wait()
-    acc_g[...] = dot(rows_t[my_c], wg_v[my_c])
-    acc_u[...] = dot(rows_t[my_c], wu_v[my_c])
-
-    @pl.loop(1, gw)
-    def _(i):
-        c = ring_back(i)
-        bt_copy(my_c, c).wait_recv()
+    @pl.loop(1, chips)
+    def _(i):
+        c = near(i)
+        bg_copy(c, my_c, c).start()
+
+    bg_copy(sib, my_c, sib).start()
+
+    def gate_up(c):
         wg_copy(c).wait()
         wu_copy(c).wait()
         x = rows_t[c]
         acc_g[...] += dot(x, wg_v[c])
         acc_u[...] += dot(x, wu_v[c])
 
+    acc_g[...] = jnp.zeros_like(acc_g)
+    acc_u[...] = jnp.zeros_like(acc_u)
+    gate_up(my_c)
+    bt_copy(my_c, sib, sib).wait_recv()
+    gate_up(sib)
+
+    @pl.loop(1, chips)
+    def _(i):
+        c = near_back(i)
+        bt_copy(my_c, c, c).wait_recv()
+        bt_copy(sib, c, twin(c)).start()
+        gate_up(c)
+
+    @pl.loop(1, chips)
+    def _(i):
+        c = near_back(i)
+        bg_copy(my_c, c, c).wait_recv()
+        bg_copy(sib, c, twin(c)).start()
+        bt_copy(my_c, twin(c), c).wait_recv()
+        gate_up(twin(c))
+
     pre_gate = acc_g[...]
     hidden = (pre_gate * jax.nn.sigmoid(pre_gate) * acc_u[...]).astype(BF16)
 
+    def sv_copy(c, at):
+        return remote(rs_send_v.at[c], sib_v.at[at], rv_ss.at[c], sv_rs.at[at], base + sib)
+
     def rv_copy(to, at):
         return remote(rs_send_v.at[to], rs_v.at[at], rv_ss.at[to], rv_rs.at[at], base + to)
 
+    def sg_copy(c, at):
+        return remote(rs_send_g.at[c], sib_g.at[at], rg_ss.at[c], sg_rs.at[at], base + sib)
+
     def rg_copy(to, at):
         return remote(rs_send_g.at[to], rs_g.at[at], rg_ss.at[to], rg_rs.at[at], base + to)
 
     gg_acc[...] = jnp.zeros_like(gg_acc)
 
-    @pl.loop(1, gw)
-    def _(i):
-        c = ring(i)
-        bg_copy(my_c, c).wait_recv()
+    @pl.loop(1, chips + 1)
+    def _(i):
+        c = twin(near(i))
+        bg_copy(my_c, c, c).wait_recv()
         wd_copy(c).wait()
         value = dot(hidden, wd_v[c])
         rs_send_v[c] = value.astype(BF16)
-        rv_copy(c, my_c).start()
+        sv_copy(c, c // 2).start()
         gg_acc[...] += value * rows_g[c].astype(F32)
+
+    @pl.loop(1, chips)
+    def _(i):
+        c = near(i)
+        wd_copy(c).wait()
+        value = dot(hidden, wd_v[c])
+        gg_acc[...] += value * rows_g[c].astype(F32)
+        sv_copy(c, c // 2).wait_recv()
+        rs_send_v[c] = (value + sib_v[c // 2].astype(F32)).astype(BF16)
+        rv_copy(c, my_chip).start()
 
     wd_copy(my_c).wait()
     value = dot(hidden, wd_v[my_c])
-    rs_v[my_c] = value.astype(BF16)
+    sv_copy(my_c, my_chip).wait_recv()
+    rs_v[my_chip] = (value + sib_v[my_chip].astype(F32)).astype(BF16)
     terms = live * jnp.sum(gg_acc[...] + value * rows_g[my_c].astype(F32), axis=1, keepdims=True)
     wide = iota((cap, capl), 0) == iota((cap, capl), 1)
     gg_send[...] = jnp.broadcast_to(jnp.sum(jnp.where(wide, terms, 0.0), axis=0, keepdims=True), gg_send.shape)
@@ -265,7 +316,7 @@
         buf[...] = slots
 
     def summed(buf):
-        return lax.fori_loop(1, gw, lambda c, s: s + buf[c].astype(F32), buf[0].astype(F32))
+        return lax.fori_loop(1, chips, lambda c, s: s + buf[c].astype(F32), buf[0].astype(F32))
 
     def ov_copy(to, at):
         return remote(own_send_v.at[to], own_v.at[at], ov_ss.at[to], ov_rs.at[at], to)
@@ -273,9 +324,9 @@
     def og_copy(to, at):
         return remote(own_send_g.at[to], own_g.at[at], og_ss.at[to], og_rs.at[at], to)
 
-    @pl.loop(1, gw)
-    def _(i):
-        rv_copy(my_c, ring_back(i)).wait_recv()
+    @pl.loop(1, chips)
+    def _(i):
+        rv_copy(my_c, near_back(i) // 2).wait_recv()
 
     to_owners(weight * summed(rs_v), own_send_v)
 
@@ -285,17 +336,30 @@
 
     own_v[me] = own_send_v[me]
 
-    @pl.loop(1, gw)
-    def _(i):
-        c = ring(i)
-        rs_send_g[c] = (dot_nt(d_gate, wg_v[c]) + dot_nt(d_up, wu_v[c])).astype(BF16)
-        rg_copy(c, my_c).start()
-
-    rs_g[my_c] = (dot_nt(d_gate, wg_v[my_c]) + dot_nt(d_up, wu_v[my_c])).astype(BF16)
-
-    @pl.loop(1, gw)
-    def _(i):
-        rg_copy(my_c, ring_back(i)).wait_recv()
+    def token_part(c):
+        return dot_nt(d_gate, wg_v[c]) + dot_nt(d_up, wu_v[c])
+
+    @pl.loop(1, chips + 1)
+    def _(i):
+        c = twin(near(i))
+        rs_send_g[c] = token_part(c).astype(BF16)
+        sg_copy(c, c // 2).start()
+
+    @pl.loop(1, chips)
+    def _(i):
+        c = near(i)
+        part = token_part(c)
+        sg_copy(c, c // 2).wait_recv()
+        rs_send_g[c] = (part + sib_g[c // 2].astype(F32)).astype(BF16)
+        rg_copy(c, my_chip).start()
+
+    part = token_part(my_c)
+    sg_copy(my_c, my_chip).wait_recv()
+    rs_g[my_chip] = (part + sib_g[my_chip].astype(F32)).astype(BF16)
+
+    @pl.loop(1, chips)
+    def _(i):
+        rg_copy(my_c, near_back(i) // 2).wait_recv()
 
     to_owners(summed(rs_g), own_send_g)
 
@@ -316,7 +380,7 @@
         def _(c):
             rows = jnp.concatenate([unpack(buf[e * gw + c]) for e in range(experts)], axis=0)
             cols = pl.ds(pl.multiple_of(c * chunk, chunk), chunk)
-            ref[:, cols] = dot(spread, rows.astype(BF16)).astype(BF16)
+            ref[:, cols] = rows.astype(BF16)
 
     @pl.loop(1, n)
     def _(i):
@@ -348,11 +412,18 @@
 
     @pl.loop(1, gw)
     def _(i):
-        to = ring(i)
-        bt_copy(to, my_c).wait_send()
-        bg_copy(to, my_c).wait_send()
-        rv_copy(to, my_c).wait_send()
-        rg_copy(to, my_c).wait_send()
+        c = ring(i)
+        bt_copy(c, my_c, c).wait_send()
+        bg_copy(c, my_c, c).wait_send()
+        rv_copy(c, my_chip).wait_send()
+        rg_copy(c, my_chip).wait_send()
+
+
+def expand(spread_ref, value_ref, grad_ref, gg_in, out_ref, tg_ref, gg_ref):
+    spread = spread_ref[...]
+    out_ref[...] = dot(spread, value_ref[...]).astype(BF16)
+    tg_ref[...] = dot(spread, grad_ref[...]).astype(BF16)
+    gg_ref[...] = gg_in[...]
 
 
 def shards(tokens, cotangent, gate_weight, up_weight, down_weight, chosen, counts, gate_values):
@@ -369,15 +440,16 @@
     vmem = pl.BlockSpec(memory_space=pltpu.VMEM)
     hbm = pl.BlockSpec(memory_space=pl.ANY)
     dma = pltpu.SemaphoreType.DMA
-    return pl.pallas_call(
+    value, grad, spread, gg = pl.pallas_call(
         functools.partial(kernel, n, experts, packed),
         out_shape=(
-            jax.ShapeDtypeStruct((tok, d), BF16),
-            jax.ShapeDtypeStruct((tok, d), BF16),
+            jax.ShapeDtypeStruct((experts * SLOT, d), BF16),
+            jax.ShapeDtypeStruct((experts * SLOT, d), BF16),
+            jax.ShapeDtypeStruct((tok, experts * SLOT), BF16),
             jax.ShapeDtypeStruct((experts, cap), F32),
         ),
         in_specs=[hbm] * 5 + [vmem, pl.BlockSpec(memory_space=pltpu.SMEM), vmem],
-        out_specs=(vmem, vmem, vmem),
+        out_specs=(vmem, vmem, vmem, vmem),
         scratch_shapes=[
             pltpu.VMEM((tok, d), BF16),
             pltpu.VMEM((tok, d), BF16),
@@ -394,8 +466,10 @@
             pltpu.VMEM((cap, chunk), F32),
             pltpu.VMEM((gw, cap, chunk), BF16),
             pltpu.VMEM((gw, cap, chunk), BF16),
-            pltpu.VMEM((gw, cap, chunk), BF16),
-            pltpu.VMEM((gw, cap, chunk), BF16),
+            pltpu.VMEM((gw // 2, cap, chunk), BF16),
+            pltpu.VMEM((gw // 2, cap, chunk), BF16),
+            pltpu.VMEM((gw // 2, cap, chunk), BF16),
+            pltpu.VMEM((gw // 2, cap, chunk), BF16),
             pltpu.VMEM(own_shape, own_type),
             pltpu.VMEM(own_shape, own_type),
             pltpu.VMEM(own_shape, own_type),
@@ -405,7 +479,7 @@
             dma((2,)), dma((gw,)), dma((gw,)), dma((gw,)),
             dma((n,)), dma((n,)),
             dma((gw,)), dma((gw,)), dma((gw,)), dma((gw,)),
-            dma((gw,)), dma((gw,)), dma((gw,)), dma((gw,)),
+            dma((gw,)), dma((gw // 2,)), dma((gw // 2,)), dma((gw,)), dma((gw // 2,)), dma((gw // 2,)),
             dma((n,)), dma((n,)), dma((n,)), dma((n,)), dma((n,)), dma((n,)),
         ],
         compiler_params=pltpu.CompilerParams(
@@ -413,6 +487,24 @@
         ),
         name="expert_layer",
     )(tokens, cotangent, gate_weight, up_weight, down_weight, chosen, counts, gate_values)
+    steps = 4
+    part = d // steps
+    whole = pl.BlockSpec((tok, experts * SLOT), lambda i: (0, 0))
+    rows = pl.BlockSpec((experts * SLOT, part), lambda i: (0, i))
+    wide = pl.BlockSpec((tok, part), lambda i: (0, i))
+    small = pl.BlockSpec((experts, cap), lambda i: (0, 0))
+    return pl.pallas_call(
+        expand,
+        grid=(steps,),
+        out_shape=(
+            jax.ShapeDtypeStruct((tok, d), BF16),
+            jax.ShapeDtypeStruct((tok, d), BF16),
+            jax.ShapeDtypeStruct((experts, cap), F32),
+        ),
+        in_specs=[whole, rows, rows, small],
+        out_specs=(wide, wide, small),
+        name="expand_rows",
+    )(spread, value, grad, gg)
 
 
 def solution(mesh):

time: 62.3 us -> 53.3 us (0.86)
  local copies, waits for them, and re-layouts: 5.8 us -> 0 us
  Pallas kernels: 55.6 us -> 52.3 us
    pallas_call x1, Pallas kernels: 55.6 us -> 48.7 us  [shards(): pl.pallas_call(functools.partial(kernel, n, experts, packed), out_shape=(...]
    unnamed x3 -> x0, local copies, waits for them, and re-layouts: 5.8 us -> none
    pallas_call x0 -> x1, Pallas kernels: none -> 3.58 us  [shards(): pl.pallas_call(expand, grid=(steps,), out_shape=(jax.ShapeDtypeStruct((to...]
where the time goes in v2:
time: 53.3 us; the launch traced here: 52.9 us
  Pallas kernels  52.3 us (98%)
  between operations  0.64 us (1%)
    pallas_call x1, Pallas kernels, shards(): pl.pallas_call(functools.partial(kernel, n, experts, packed), out_shape=(...  48.7 us
    pallas_call x1, Pallas kernels, shards(): pl.pallas_call(expand, grid=(steps,), out_shape=(jax.ShapeDtypeStruct((to...  3.58 us

profile of v2, /device:TPU:0, one launch (start us, length us, event | category | flops | bytes accessed | tf_op | source)
XLA Modules:
  0.0 52.9 jit_solution(13132379838727039781)
XLA Ops:
  0.6 48.7 %expert_layer.1 = (bf16[16,4096]{1,0:T(8,128)(2,1)}, bf16[16,4096]{1,0:T(8,128)(2,1)}, bf16[128,16]{1,0:T(8,128)(2,1)}, f32[2,64]{1,0:T(2,128)}) custom-call(bf16[128,4096]{1,0:T(8,128)(2,1)} %tok_hbm.1, bf16[128,4096]{1,0:T(8,128)(2,1)} %cot_hbm.1, bf16[4096,1024]{1,0:T(8,128)(2,1)} %wg_hbm.1, bf16[4096,1024]{1,0:T(8,128)(2,1)} %wu_hbm.1, ...), custom_call_target="tpu_custom_call" | custom-call | tf_op jit(solution)/shard_map/expert_layer/pallas_call | solution.py:443
  49.3 3.6 %expand_rows.1 = (bf16[128,4096]{1,0:T(8,128)(2,1)}, bf16[128,4096]{1,0:T(8,128)(2,1)}, f32[2,64]{1,0:T(2,128)}) custom-call(bf16[128,16]{1,0:T(8,128)(2,1)} %get-tuple-element.7.spread_ref, bf16[16,4096]{1,0:T(8,128)(2,1)} %get-tuple-element.8.value_ref, bf16[16,4096]{1,0:T(8,128)(2,1)} %get-tuple-element.9.grad_ref, f32[2,64]{1,0:T(2,128)} %get-tuple-element.10.gg_in), custom_call_target="tpu_custom_call" | custom-call | tf_op jit(solution)/shard_map/expand_rows/pallas_call | solution.py:496

commit v3 on v2

--- a/solution.py
+++ b/solution.py
@@ -52,6 +52,7 @@
     chunk = rows_t.shape[2]
     cap = rows_t.shape[1]
     capl = gg_send.shape[1]
+    flat = chips <= 4
 
     def other(i):
         return lax.rem(me + i, n)
@@ -136,7 +137,7 @@
     tok_copy.wait()
     cot_copy.wait()
 
-    @pl.loop(0, gw)
+    @pl.loop(0, gw, unroll=flat)
     def _(c):
         cols = pl.ds(pl.multiple_of(c * chunk, chunk), chunk)
         t = dot(pick, tok_v[:, cols])
@@ -198,7 +199,7 @@
     def bg_copy(to, at, sem):
         return remote(rows_g.at[at], rows_g.at[at], bg_ss.at[sem], bg_rs.at[at], base + to)
 
-    @pl.loop(1, chips)
+    @pl.loop(1, chips, unroll=flat)
     def _(i):
         c = near(i)
         bt_copy(c, my_c, c).start()
@@ -206,7 +207,7 @@
     bt_copy(sib, my_c, sib).start()
     rows_g[my_c] = dot(from_g, arrived).astype(BF16)
 
-    @pl.loop(1, chips)
+    @pl.loop(1, chips, unroll=flat)
     def _(i):
         c = near(i)
         bg_copy(c, my_c, c).start()
@@ -226,14 +227,14 @@
     bt_copy(my_c, sib, sib).wait_recv()
     gate_up(sib)
 
-    @pl.loop(1, chips)
+    @pl.loop(1, chips, unroll=flat)
     def _(i):
         c = near_back(i)
         bt_copy(my_c, c, c).wait_recv()
         bt_copy(sib, c, twin(c)).start()
         gate_up(c)
 
-    @pl.loop(1, chips)
+    @pl.loop(1, chips, unroll=flat)
     def _(i):
         c = near_back(i)
         bg_copy(my_c, c, c).wait_recv()
@@ -258,7 +259,7 @@
 
     gg_acc[...] = jnp.zeros_like(gg_acc)
 
-    @pl.loop(1, chips + 1)
+    @pl.loop(1, chips + 1, unroll=flat)
     def _(i):
         c = twin(near(i))
         bg_copy(my_c, c, c).wait_recv()
@@ -268,7 +269,7 @@
         sv_copy(c, c // 2).start()
         gg_acc[...] += value * rows_g[c].astype(F32)
 
-    @pl.loop(1, chips)
+    @pl.loop(1, chips, unroll=flat)
     def _(i):
         c = near(i)
         wd_copy(c).wait()
@@ -289,18 +290,15 @@
     def q_copy(to, at):
         return remote(gg_send, gg_land.at[at], q_ss.at[to], q_rs.at[at], to)
 
-    @pl.loop(1, n)
-    def _(i):
-        q_copy(other(i), me).start()
-
-    gg_land[me] = gg_send[...]
-
     acc_b[...] = jnp.zeros_like(acc_b)
 
-    @pl.loop(0, gw)
-    def _(c):
+    def back_part(c):
         scaled = (weight * rows_g[c].astype(F32)).astype(BF16)
-        acc_b[...] += dot_nt(scaled, wd_v[c])
+        return dot_nt(scaled, wd_v[c])
+
+    @pl.loop(0, chips, unroll=flat)
+    def _(p):
+        acc_b[...] += back_part(2 * p) + back_part(2 * p + 1)
 
     up = acc_u[...]
     sig = jax.nn.sigmoid(pre_gate)
@@ -316,7 +314,7 @@
         buf[...] = slots
 
     def summed(buf):
-        return lax.fori_loop(1, chips, lambda c, s: s + buf[c].astype(F32), buf[0].astype(F32))
+        return lax.fori_loop(1, chips, lambda c, s: s + buf[c].astype(F32), buf[0].astype(F32), unroll=flat)
 
     def ov_copy(to, at):
         return remote(own_send_v.at[to], own_v.at[at], ov_ss.at[to], ov_rs.at[at], to)
@@ -324,28 +322,16 @@
     def og_copy(to, at):
         return remote(own_send_g.at[to], own_g.at[at], og_ss.at[to], og_rs.at[at], to)
 
-    @pl.loop(1, chips)
-    def _(i):
-        rv_copy(my_c, near_back(i) // 2).wait_recv()
-
-    to_owners(weight * summed(rs_v), own_send_v)
-
-    @pl.loop(1, n)
-    def _(i):
-        ov_copy(other(i), me).start()
-
-    own_v[me] = own_send_v[me]
-
     def token_part(c):
         return dot_nt(d_gate, wg_v[c]) + dot_nt(d_up, wu_v[c])
 
-    @pl.loop(1, chips + 1)
+    @pl.loop(1, chips + 1, unroll=flat)
     def _(i):
         c = twin(near(i))
         rs_send_g[c] = token_part(c).astype(BF16)
         sg_copy(c, c // 2).start()
 
-    @pl.loop(1, chips)
+    @pl.loop(1, chips, unroll=flat)
     def _(i):
         c = near(i)
         part = token_part(c)
@@ -357,7 +343,25 @@
     sg_copy(my_c, my_chip).wait_recv()
     rs_g[my_chip] = (part + sib_g[my_chip].astype(F32)).astype(BF16)
 
-    @pl.loop(1, chips)
+    @pl.loop(1, chips, unroll=flat)
+    def _(i):
+        rv_copy(my_c, near_back(i) // 2).wait_recv()
+
+    to_owners(weight * summed(rs_v), own_send_v)
+
+    @pl.loop(1, n)
+    def _(i):
+        ov_copy(other(i), me).start()
+
+    own_v[me] = own_send_v[me]
+
+    @pl.loop(1, n)
+    def _(i):
+        q_copy(other(i), me).start()
+
+    gg_land[me] = gg_send[...]
+
+    @pl.loop(1, chips, unroll=flat)
     def _(i):
         rg_copy(my_c, near_back(i) // 2).wait_recv()
 
@@ -376,7 +380,7 @@
         return x
 
     def finish(buf, ref):
-        @pl.loop(0, gw)
+        @pl.loop(0, gw, unroll=flat)
         def _(c):
             rows = jnp.concatenate([unpack(buf[e * gw + c]) for e in range(experts)], axis=0)
             cols = pl.ds(pl.multiple_of(c * chunk, chunk), chunk)
@@ -487,7 +491,7 @@
         ),
         name="expert_layer",
     )(tokens, cotangent, gate_weight, up_weight, down_weight, chosen, counts, gate_values)
-    steps = 4
+    steps = 2
     part = d // steps
     whole = pl.BlockSpec((tok, experts * SLOT), lambda i: (0, 0))
     rows = pl.BlockSpec((experts * SLOT, part), lambda i: (0, i))

time: 53.3 us -> 50.9 us (0.955)
  Pallas kernels: 52.3 us -> 50.1 us
    pallas_call x1, Pallas kernels: 48.7 us -> 47.5 us  [shards(): pl.pallas_call(functools.partial(kernel, n, experts, packed), out_shape=(...]
    pallas_call x1, Pallas kernels: 3.58 us -> 2.56 us  [shards(): pl.pallas_call(expand, grid=(steps,), out_shape=(jax.ShapeDtypeStruct((to...]
where the time goes in v3:
time: 50.9 us; the launch traced here: 50.7 us
  Pallas kernels  50.1 us (98%)
  between operations  0.64 us (1%)
    pallas_call x1, Pallas kernels, shards(): pl.pallas_call(functools.partial(kernel, n, experts, packed), out_shape=(...  47.5 us
    pallas_call x1, Pallas kernels, shards(): pl.pallas_call(expand, grid=(steps,), out_shape=(jax.ShapeDtypeStruct((to...  2.56 us

profile of v3, /device:TPU:0, one launch (start us, length us, event | category | flops | bytes accessed | tf_op | source)
XLA Modules:
  0.0 50.7 jit_solution(12060499848119424868)
XLA Ops:
  0.6 47.5 %expert_layer.1 = (bf16[16,4096]{1,0:T(8,128)(2,1)}, bf16[16,4096]{1,0:T(8,128)(2,1)}, bf16[128,16]{1,0:T(8,128)(2,1)}, f32[2,64]{1,0:T(2,128)}) custom-call(bf16[128,4096]{1,0:T(8,128)(2,1)} %tok_hbm.1, bf16[128,4096]{1,0:T(8,128)(2,1)} %cot_hbm.1, bf16[4096,1024]{1,0:T(8,128)(2,1)} %wg_hbm.1, bf16[4096,1024]{1,0:T(8,128)(2,1)} %wu_hbm.1, ...), custom_call_target="tpu_custom_call" | custom-call | tf_op jit(solution)/shard_map/expert_layer/pallas_call | solution.py:447
  48.2 2.6 %expand_rows.1 = (bf16[128,4096]{1,0:T(8,128)(2,1)}, bf16[128,4096]{1,0:T(8,128)(2,1)}, f32[2,64]{1,0:T(2,128)}) custom-call(bf16[128,16]{1,0:T(8,128)(2,1)} %get-tuple-element.7.spread_ref, bf16[16,4096]{1,0:T(8,128)(2,1)} %get-tuple-element.8.value_ref, bf16[16,4096]{1,0:T(8,128)(2,1)} %get-tuple-element.9.grad_ref, f32[2,64]{1,0:T(2,128)} %get-tuple-element.10.gg_in), custom_call_target="tpu_custom_call" | custom-call | tf_op jit(solution)/shard_map/expand_rows/pallas_call | solution.py:500
